TPU v7x, 32 devices: a whole 2x2x4 slice. The times are simulated.
32 devices in a mesh: groups: 2 (over y), bucket: 4 (over z), rel: 2 (over x), sub: 2 (over core).
Axes of the slice: x: 2, y: 2, z: 4, core: 2. Of those that a mesh axis runs over, the one named last changes fastest.
Arguments:
- entity: float32 [2048, 256], P(('groups', 'bucket')), parts along dimension 0, may hold values from -2.5 to 2.5
- entity_acc: float32 [2048], P(('groups', 'bucket')), parts along dimension 0, may hold values from 0.01 to 1
- relation: float32 [2048, 256], P(('groups', 'rel')), parts along dimension 0, may hold values from -4 to 4
- relation_acc: float32 [2048], P(('groups', 'rel')), parts along dimension 0, may hold values from 0.01 to 1
- edge_src: int32 [8, 2, 1, 1024], P(('groups', 'bucket'), 'rel'), parts along dimension 0, may hold values from 0 to 255
- edge_dst: int32 [8, 2, 1, 1024], P(('groups', 'bucket'), 'rel'), parts along dimension 0, may hold values from 0 to 255
- edge_rel: int32 [8, 2, 1, 1024], P(('groups', 'bucket'), 'rel'), parts along dimension 0, may hold values from 0 to 511
- negatives: int32 [8, 2, 1, 1024], P(('groups', 'bucket'), 'rel', None, 'sub'), parts along dimension 0, may hold values from 0 to 255
- ovf_src: int32 [8, 2, 2, 8, 128], P(('groups', 'bucket'), 'rel', 'sub'), parts along dimension 0, may hold values from 0 to 255
- ovf_dst: int32 [8, 2, 2, 8, 128], P(('groups', 'bucket'), 'rel', 'sub'), parts along dimension 0, may hold values from 0 to 255
- ovf_rel: int32 [8, 2, 2, 8, 128], P(('groups', 'bucket'), 'rel', 'sub'), parts along dimension 0, may hold values from 0 to 511
- ovf_count: int32 [4, 2, 4], P(('groups', 'rel'), 'sub'), parts along dimension 0, may hold values from 1 to 8, 16 in all within a row
Outputs:
- new_entity: float32 [2048, 256], P(('groups', 'bucket')), parts along dimension 0
- new_entity_acc: float32 [2048], P(('groups', 'bucket')), parts along dimension 0
- new_relation: float32 [2048, 256], P(('groups', 'rel')), parts along dimension 0
- new_relation_acc: float32 [2048], P(('groups', 'rel')), parts along dimension 0
There are 2 independent parts, one for each index of `groups`. A program takes and returns all parts, laid end to end along the dimension named above; each array names one. Nothing has to cross between parts.
Inputs may be any that keep to these rules, and one draw needn't show every extreme that they name: `ovf_count`: for each relation group and sub index, the counts over the 4 buckets sum to 16, and the largest of them is 8.
All inputs are finite; a program needn't handle non-finite values.
Results may differ from a plain program's by a relative error of at most 0.0001.
Values sent between devices are 32-bit elements; how exact they have to be, the bound alone decides.
A program may use at most 64 MiB of HBM per device.

v0:
```python
import jax
import jax.numpy as jnp
from jax import lax
from jax.sharding import PartitionSpec as P

NEG = 1024


HI = lax.Precision.HIGHEST


def shifted(value, axis, steps):
    count = lax.axis_size(axis)
    pairs = [(source, (source + steps) % count) for source in range(count)]
    return lax.ppermute(value, axis, pairs)


def block_grads(q, dst_rows, neg_rows, pos_weight):
    pos = jnp.sum(q * dst_rows, axis=-1)
    scores = jnp.dot(q, neg_rows.T, precision=HI)
    dpos = -jax.nn.sigmoid(-pos) * pos_weight
    dneg = jax.nn.sigmoid(scores) * (1.0 / NEG)
    dq = dpos[:, None] * dst_rows + jnp.dot(dneg, neg_rows, precision=HI)
    ddst = dpos[:, None] * q
    dnegrows = lax.dot_general(dneg, q, (((0,), (0,)), ((), ())), precision=HI)
    return (dq, ddst, dnegrows)


def spill_grads(queries, dests, live):
    edges = queries.shape[1]
    scores = jnp.einsum("mid,mkd->mik", queries, dests, precision=HI)
    pos = jnp.sum(queries * dests, axis=-1)
    ident = jnp.eye(edges, dtype=jnp.float32)
    dscore = (
        jax.nn.sigmoid(scores) * (1.0 / edges) + ident[None] * (-jax.nn.sigmoid(-pos))[:, :, None]
    )
    dscore = dscore * live[:, None, None]
    dq = jnp.einsum("mik,mkd->mid", dscore, dests, precision=HI)
    ddst = jnp.einsum("mik,mid->mkd", dscore, queries, precision=HI)
    return (dq, ddst)


def adagrad(table, accum, grad):
    fresh = accum + jnp.mean(grad * grad, axis=-1)
    return (table - 0.1 * grad / jnp.sqrt(fresh)[:, None], fresh)


def body(
    entity,
    entity_acc,
    relation,
    relation_acc,
    edge_src,
    edge_dst,
    edge_rel,
    negatives,
    ovf_src,
    ovf_dst,
    ovf_rel,
    ovf_count,
):
    n_bucket = lax.axis_size("bucket")
    n_sub = lax.axis_size("sub")
    ent_rows, width = entity.shape
    dst_tab = shifted(entity, "bucket", -1)
    gsrc = jnp.zeros((ent_rows, width), jnp.float32)
    gdst = jnp.zeros((ent_rows, width), jnp.float32)
    grel = jnp.zeros(relation.shape, jnp.float32)
    s_ids = edge_src[0, 0, 0]
    d_ids = edge_dst[0, 0, 0]
    r_ids = edge_rel[0, 0, 0]
    n_ids = negatives[0, 0, 0]
    src_rows = entity[s_ids]
    rel_rows = relation[r_ids]
    dq, ddst, dneg = block_grads(src_rows * rel_rows, dst_tab[d_ids], dst_tab[n_ids], 1.0 / n_sub)
    gsrc = gsrc.at[s_ids].add(dq * rel_rows)
    grel = grel.at[r_ids].add(dq * src_rows)
    gdst = gdst.at[d_ids].add(ddst).at[n_ids].add(dneg)
    o_src = ovf_src[0, 0, 0]
    o_dst = ovf_dst[0, 0, 0]
    o_rel = ovf_rel[0, 0, 0]
    spill = o_src.shape[0]
    counts = ovf_count[0, 0]
    my_bucket = lax.axis_index("bucket")
    peers = jnp.arange(n_bucket, dtype=jnp.int32)
    own = jnp.sum(jnp.where(peers == my_bucket, counts, 0))
    order = jnp.arange(spill, dtype=jnp.int32)
    live = (order < own).astype(jnp.float32)
    src_rows = entity[o_src]
    rel_rows = relation[o_rel]
    queries = src_rows * rel_rows
    dests = dst_tab[o_dst]
    dq_spill, dd_spill = spill_grads(queries, dests, live)
    gsrc = gsrc.at[o_src.reshape(-1)].add((dq_spill * rel_rows).reshape(-1, width))
    grel = grel.at[o_rel.reshape(-1)].add((dq_spill * src_rows).reshape(-1, width))
    gdst = gdst.at[o_dst.reshape(-1)].add(dd_spill.reshape(-1, width))
    rel_total = lax.psum(grel, ("bucket", "sub"))
    new_relation, new_relation_acc = adagrad(relation, relation_acc, rel_total)
    share_src, share_dst = (
        lax.psum_scatter(gsrc, ("rel", "sub"), scatter_dimension=0, tiled=True),
        lax.psum_scatter(gdst, ("rel", "sub"), scatter_dimension=0, tiled=True),
    )
    arrived = shifted(share_dst, "bucket", 1)
    share_rows = share_src.shape[0]
    start = lax.axis_index(("rel", "sub")) * share_rows
    own_rows = lax.dynamic_slice_in_dim(entity, start, share_rows, 0)
    own_acc = lax.dynamic_slice_in_dim(entity_acc, start, share_rows, 0)
    part_rows, part_acc = adagrad(own_rows, own_acc, share_src + arrived)
    new_entity, new_entity_acc = (
        lax.all_gather(part_rows, ("rel", "sub"), axis=0, tiled=True),
        lax.all_gather(part_acc, ("rel", "sub"), axis=0, tiled=True),
    )
    return (new_entity, new_entity_acc, new_relation, new_relation_acc)


def solution(mesh):
    placed = (
        P(("groups", "bucket"), None),
        P(("groups", "bucket")),
        P(("groups", "rel"), None),
        P(("groups", "rel")),
        P(("groups", "bucket"), "rel", None, None),
        P(("groups", "bucket"), "rel", None, None),
        P(("groups", "bucket"), "rel", None, None),
        P(("groups", "bucket"), "rel", None, "sub"),
        P(("groups", "bucket"), "rel", "sub", None, None),
        P(("groups", "bucket"), "rel", "sub", None, None),
        P(("groups", "bucket"), "rel", "sub", None, None),
        P(("groups", "rel"), "sub", None),
    )
    return jax.shard_map(
        body,
        mesh=mesh,
        in_specs=placed,
        out_specs=(
            P(("groups", "bucket"), None),
            P(("groups", "bucket")),
            P(("groups", "rel"), None),
            P(("groups", "rel")),
        ),
        check_vma=False,
    )
```

profile of v0, /device:TPU:1, one launch (start us, length us, event | category | flops | bytes accessed | tf_op | source)
XLA Modules:
  0.0 175.2 jit_solution(11416964223847683237)
XLA Ops:
  8.0 0.0 all-reduce.3.cloned.1.call-start
  8.0 4.2 %collective-permute-start = (f32[256,256]{1,0:T(8,128)}, f32[256,256]{1,0:T(8,128)S(1)}, u32[]{:S(2)}, u32[]{:S(2)}) collective-permute-start(f32[256,256]{1,0:T(8,128)} %param.12), channel_id=1, source_target_pairs={{0,12},{4,0},{8,4},{12,8},{1,13},{5,1},{9,5},{13,9},{2,14},{6,2},{... | collective-permute-start | bytes 786440 | tf_op jit(solution)/shard_map/ppermute | solution.py:15
  12.3 0.7 compare_select_fusion.6
  13.0 0.7 compare_select_fusion.5
  13.7 0.7 compare_select_fusion.3
  14.4 0.7 compare_select_fusion.4
  15.1 0.7 fusion.20
  15.8 0.7 compare_select_fusion
  16.5 0.7 fusion.18
  17.1 0.7 fusion.22
  17.8 1.3 fusion.23
  19.1 0.6 compare_convert_fusion
  19.8 0.0 copy-start.2
  19.8 5.7 %gather_fusion = f32[1024,256]{1,0:T(8,128)} fusion(f32[256,256]{1,0:T(8,128)} %param.12, s32[1024]{0:T(1024)S(1)} %broadcast_clamp_fusion.2), kind=kCustom, calls=%fused_computation | custom fusion | bytes 2101248 | tf_op jit(solution)/shard_map/gather | solution.py:73
  25.5 3.5 %gather_fusion.1 = f32[1024,256]{1,0:T(8,128)S(1)} fusion(f32[512,256]{1,0:T(8,128)S(1)} %copy-done.2, s32[1024]{0:T(1024)S(1)} %broadcast_clamp_fusion), kind=kCustom, calls=%fused_computation.1 | custom fusion | bytes 2101248 | tf_op jit(solution)/shard_map/gather | solution.py:74
  28.9 0.0 copy-start
  29.0 4.7 %gather_fusion.5 = f32[1024,256]{1,0:T(8,128)} fusion(f32[512,256]{1,0:T(8,128)S(1)} %copy-done.2, s32[1024]{0:T(1024)S(1)} %fusion.20), kind=kCustom, calls=%fused_computation.5 | custom fusion | bytes 2101248 | tf_op jit(solution)/shard_map/gather | solution.py:90
  33.6 4.7 %gather_fusion.4 = f32[1024,256]{1,0:T(8,128)} fusion(f32[256,256]{1,0:T(8,128)S(1)} %copy-done, s32[1024]{0:T(1024)S(1)} %fusion.18), kind=kCustom, calls=%fused_computation.4 | custom fusion | bytes 2101248 | tf_op jit(solution)/shard_map/gather | solution.py:89
  38.3 3.5 %gather_fusion.2 = f32[1024,256]{1,0:T(8,128)S(1)} fusion(f32[256,256]{1,0:T(8,128)S(1)} %collective-permute-done, s32[1024]{0:T(1024)S(1)} %broadcast_clamp_fusion.1), kind=kCustom, calls=%fused_computation.2 | custom fusion | bytes 2101248 | tf_op jit(solution)/shard_map/gather | solution.py:75
  41.8 2.4 %multiply_reduce_fusion.1 = (f32[1024]{0:T(1024)S(1)}, f32[1024,256]{1,0:T(8,128)}) fusion(f32[1024,256]{1,0:T(8,128)S(1)} %gather_fusion.2, f32[1024,256]{1,0:T(8,128)} %gather_fusion, f32[1024,256]{1,0:T(8,128)S(1)} %gather_fusion.1), kind=kLoop, calls=%fused_computation.30 | loop fusion | flops 785408 | bytes 4198400 | tf_op jit(solution)/shard_map/reduce_sum | solution.py:19
  44.2 2.2 %gather_fusion.3 = f32[512,256]{1,0:T(8,128)} fusion(f32[256,256]{1,0:T(8,128)S(1)} %collective-permute-done, s32[1024]{0:T(1024)S(1)} %pad_clamp_fusion), kind=kCustom, calls=%fused_computation.3 | custom fusion | bytes 1050624 | tf_op jit(solution)/shard_map/gather | solution.py:75
  46.4 3.2 %divide_multiply_fusion = f32[1024,512]{1,0:T(8,128)S(1)} fusion(f32[1024,256]{1,0:T(8,128)S(1)} %copy-done.7, f32[512,256]{1,0:T(8,128)} %gather_fusion.3), kind=kOutput, calls=%fused_computation.14 | convolution fusion | flops 1612709888 | bytes 3670016 | tf_op jit(solution)/shard_map/dot_general | solution.py:20
  49.6 0.0 copy-start.15
  49.6 4.4 %fusion.29 = f32[512,256]{1,0:T(8,128)} fusion(f32[1024,512]{1,0:T(8,128)S(1)} %divide_multiply_fusion, f32[1024,256]{1,0:T(8,128)S(1)} %copy-done.7), kind=kOutput, calls=%fused_computation.73 | convolution fusion | flops 1610612736 | bytes 3670016 | tf_op jit(solution)/shard_map/dot_general | solution.py:25
  54.0 2.8 %fusion.28 = f32[1024,256]{1,0:T(8,128)} fusion(f32[1024,512]{1,0:T(8,128)S(1)} %divide_multiply_fusion, f32[512,256]{1,0:T(8,128)S(1)} %copy-done.15), kind=kOutput, calls=%fused_computation.72 | convolution fusion | flops 1610612736 | bytes 3670016 | tf_op jit(solution)/shard_map/dot_general | solution.py:23
  56.8 4.7 %gather_fusion.6 = f32[1024,256]{1,0:T(8,128)} fusion(f32[256,256]{1,0:T(8,128)S(1)} %collective-permute-done, s32[1024]{0:T(1024)S(1)} %fusion.22), kind=kCustom, calls=%fused_computation.6 | custom fusion | bytes 2101248 | tf_op jit(solution)/shard_map/gather | solution.py:92
  61.5 1.8 %multiply_reduce_fusion = (f32[8,128]{1,0:T(8,128)S(1)}, f32[8,128,256]{2,1,0:T(8,128)S(1)}) fusion(f32[8,128,256]{2,1,0:T(8,128)} %bitcast.61, f32[8,128,256]{2,1,0:T(8,128)} %bitcast.59, f32[8,128,256]{2,1,0:T(8,128)S(1)} %bitcast.57), kind=kLoop, calls=%fused_computation.26 | loop fusion | flops 785408 | bytes 4198400 | tf_op jit(solution)/shard_map/reduce_sum | solution.py:32
  63.4 1.2 fusion.5
  64.6 0.4 copy-done.10
  64.9 0.3 copy-done.11
  65.3 2.5 %fusion.27 = (f32[8,128,256]{2,1,0:T(8,128)}, f32[8,128,256]{2,1,0:T(8,128)}) fusion(f32[8,128,256]{2,1,0:T(8,128)S(1)} %bitcast.60, f32[8,128,256]{2,1,0:T(8,128)S(1)} %bitcast.58, f32[8,128,128]{2,1,0:T(8,128)S(1)} %fusion.5, f32[8,128,256]{2,1,0:T(8,128)S(1)} %bitcast.63), kind=kOutput, calls=%fused_computation.71 | convolution fusion | flops 403177472 | bytes 5767168 | tf_op jit(solution)/shard_map/mik,mkd->mid/dot_general | solution.py:38
  67.8 6.6 %scatter_custom_fusion.2 = f32[256,256]{1,0:T(8,128)S(1)} fusion(s32[1024]{0:T(1024)S(1)} %bitcast.80, f32[1024,256]{1,0:T(8,128)S(1)} %copy-done.8, f32[1024]{0:T(1024)S(1)} %negate_multiply_fusion, f32[]{:T(128)} %constant.20.clone.1), kind=kCustom, calls=%fused_computation.24 | custom fusion | flops 524288 | bytes 1314820 | tf_op jit(solution)/shard_map/scatter-add | solution.py:78
  74.4 7.4 %scatter_custom_fusion.5 = f32[512,256]{1,0:T(8,128)S(1)} fusion(s32[1024]{0:T(1024)S(1)} %bitcast.78, f32[1024,256]{1,0:T(8,128)} %gather_fusion, f32[]{:T(128)} %constant.20.clone.1, f32[1024,256]{1,0:T(8,128)} %fusion.28, f32[1024,256]{1,0:T(8,128)S(1)} %gather_fusion.2, f32[1024]{0:T(1024)S(1)} %negate_multiply_fusion), kind=kCustom, calls=%fused_computation.22 | custom fusion | flops 1048576 | bytes 3674116 | tf_op jit(solution)/shard_map/scatter-add | solution.py:77
  81.8 6.8 %scatter_fusion.3 = f32[512,256]{1,0:T(8,128)S(1)} fusion(f32[512,256]{1,0:T(8,128)S(1)} %scatter_custom_fusion.5, s32[1024]{0:T(1024)S(1)} %bitcast.70, f32[1024,256]{1,0:T(8,128)} %bitcast.66), kind=kCustom, calls=%fused_computation.13 | custom fusion | flops 262144 | bytes 3149824 | tf_op jit(solution)/shard_map/scatter-add | solution.py:95
  88.6 0.8 copy-done.4
  89.4 0.0 all-reduce.3.cloned.1.call-update
  89.4 0.0 reduce-scatter.5.cloned.1.call-start
  89.5 4.2 %scatter_fusion.1 = f32[256,256]{1,0:T(8,128)S(1)} fusion(f32[256,256]{1,0:T(8,128)S(1)} %scatter_custom_fusion.2, s32[512]{0:T(512)S(1)} %bitcast.68, f32[512,256]{1,0:T(8,128)} %fusion.29), kind=kCustom, calls=%fused_computation.10 | custom fusion | flops 131072 | bytes 1574912 | tf_op jit(solution)/shard_map/scatter-add | solution.py:78
  93.7 3.1 %fusion.30 = f32[8,128,256]{2,1,0:T(8,128)} fusion(f32[8,128,128]{2,1,0:T(8,128)} %copy-done.16, f32[8,128,256]{2,1,0:T(8,128)S(1)} %copy-done.14), kind=kOutput, calls=%fused_computation.74 | convolution fusion | flops 402653184 | bytes 2621440 | tf_op jit(solution)/shard_map/mik,mid->mkd/dot_general | solution.py:39
  96.8 6.7 %scatter_fusion.2 = f32[256,256]{1,0:T(8,128)S(1)} fusion(f32[256,256]{1,0:T(8,128)S(1)} %scatter_fusion.1, s32[1024]{0:T(1024)S(1)} %bitcast.69, f32[1024,256]{1,0:T(8,128)} %bitcast.64), kind=kCustom, calls=%fused_computation.11 | custom fusion | flops 262144 | bytes 3149824 | tf_op jit(solution)/shard_map/scatter-add | solution.py:96
  103.5 0.0 copy-start.1
  103.6 0.7 copy-done.1
  104.2 0.0 reduce-scatter.5.cloned.1.call-update
  104.3 0.0 reduce-scatter.3.cloned.1.call-start
  104.3 0.6 dynamic-slice
  105.6 7.1 %scatter_custom_fusion = f32[256,256]{1,0:T(8,128)S(1)} fusion(s32[1024]{0:T(1024)S(1)} %bitcast.76, f32[1024,256]{1,0:T(8,128)S(1)} %copy-done.6, f32[1024,256]{1,0:T(8,128)} %fusion.28, f32[1024,256]{1,0:T(8,128)S(1)} %gather_fusion.2, f32[1024]{0:T(1024)S(1)} %negate_multiply_fusion, f32[]{:T(128)} %constant.20.clone.1), kind=kCustom, calls=%fused_computation.27 | custom fusion | flops 1048576 | bytes 3411972 | tf_op jit(solution)/shard_map/scatter-add | solution.py:76
  112.8 0.0 copy-start.19
  112.8 6.7 %scatter_fusion = f32[256,256]{1,0:T(8,128)S(1)} fusion(f32[256,256]{1,0:T(8,128)S(1)} %scatter_custom_fusion, s32[1024]{0:T(1024)S(1)} %bitcast.71, f32[1024,256]{1,0:T(8,128)} %bitcast.65), kind=kCustom, calls=%fused_computation.8 | custom fusion | flops 262144 | bytes 3149824 | tf_op jit(solution)/shard_map/scatter-add | solution.py:94
  119.5 0.0 copy-start.3
  119.5 0.0 copy-start.20
  119.5 0.7 copy-done.3
  120.2 0.0 reduce-scatter.3.cloned.1.call-update
  120.2 22.2 %all-reduce.3.cloned.1.call-done = f32[512,256]{1,0:T(8,128)} async-done(((f32[512,256]{1,0:T(8,128)}), f32[512,256]{1,0:T(8,128)}) %all-reduce.3.cloned.1.call-update) | async-done | bytes 524304 | tf_op jit(solution)/shard_map/psum | solution.py:97
  142.4 1.2 multiply_reduce_fusion.2
  143.6 0.6 fusion.26
  144.2 0.7 collective-permute-start.1
  144.9 2.0 %divide_subtract_fusion = f32[512,256]{1,0:T(8,128)} fusion(f32[512,256]{1,0:T(8,128)S(1)} %copy-done.2, f32[512,256]{1,0:T(8,128)} %all-reduce.3.cloned.1.call-done, f32[512]{0:T(512)S(1)} %get-tuple-element.4), kind=kLoop, calls=%fused_computation.31 | loop fusion | flops 393216 | bytes 1574912 | tf_op jit(solution)/shard_map/sub | solution.py:45
  146.9 2.5 %collective-permute-done.1 = f32[64,256]{1,0:T(8,128)S(1)} collective-permute-done((f32[64,256]{1,0:T(8,128)}, f32[64,256]{1,0:T(8,128)S(1)}, u32[]{:S(2)}, u32[]{:S(2)}) %collective-permute-start.1) | collective-permute-done | bytes 65568 | tf_op jit(solution)/shard_map/ppermute | solution.py:15
  149.3 0.9 multiply_reduce_fusion.3
  150.3 0.2 fusion.24
  150.5 9.1 %all-reduce = f32[256]{0:T(256)} all-reduce(f32[256]{0:T(256)S(1)} %get-tuple-element.12), channel_id=1, replica_groups=mesh['groups'=2,'bucket'=4,'rel'=2,'sub'=2] {'rel','sub'}, use_global_device_ids=true, to_apply=%add | all-reduce | flops 256 | bytes 2048
  159.6 0.9 divide_subtract_fusion.1
  160.6 6.5 %all_gather.6 = f32[256,256]{1,0:T(8,128)S(1)} all-gather(f32[64,256]{1,0:T(8,128)S(1)} %divide_subtract_fusion.1), channel_id=1, replica_groups=mesh['groups'=2,'bucket'=4,'rel'=2,'sub'=2] {'rel','sub'}, dimensions={0}, use_global_device_ids=true | all-gather | bytes 327680 | tf_op jit(solution)/shard_map/all_gather | solution.py:110
  167.0 0.7 copy.26
  (45 shorter events, 0.1 us)
Async XLA Ops:
  8.0 134.4 %all-reduce.3.cloned.1.call-start = ((), (), s32[]{:S(2)}) async-start(), calls=%async_computation.4 | async-start | bytes 1048576 | tf_op jit(solution)/shard_map/psum | solution.py:97
  8.0 30.3 %collective-permute-start = (f32[256,256]{1,0:T(8,128)}, f32[256,256]{1,0:T(8,128)S(1)}, u32[]{:S(2)}, u32[]{:S(2)}) collective-permute-start(f32[256,256]{1,0:T(8,128)} %param.12), channel_id=1, source_target_pairs={{0,12},{4,0},{8,4},{12,8},{1,13},{5,1},{9,5},{13,9},{2,14},{6,2},{... | collective-permute-start | bytes 786440 | tf_op jit(solution)/shard_map/ppermute | solution.py:15
  19.8 5.7 %copy-start.2 = (f32[512,256]{1,0:T(8,128)S(1)}, f32[512,256]{1,0:T(8,128)}, u32[]{:S(2)}) copy-start(f32[512,256]{1,0:T(8,128)} %param.14) | copy-start | bytes 1572868
  28.9 12.8 %copy-start.5 = (f32[1024,256]{1,0:T(8,128)}, f32[1024,256]{1,0:T(8,128)S(1)}, u32[]{:S(2)}) copy-start(f32[1024,256]{1,0:T(8,128)S(1)} %gather_fusion.1) | copy-start | bytes 3145732
  28.9 4.7 %copy-start = (f32[256,256]{1,0:T(8,128)S(1)}, f32[256,256]{1,0:T(8,128)}, u32[]{:S(2)}) copy-start(f32[256,256]{1,0:T(8,128)} %param.12) | copy-start | bytes 786436
  33.6 4.7 %copy-start.17 = (s32[1,1,1,8,128]{4,3,2,1,0:T(8,128)S(1)}, s32[1,1,1,8,128]{4,3,2,1,0:T(8,128)}, u32[]{:S(2)}) copy-start(s32[1,1,1,8,128]{4,3,2,1,0:T(8,128)} %param.21) | copy-start | bytes 12292
  44.2 2.2 %copy-start.7 = (f32[1024,256]{1,0:T(8,128)S(1)}, f32[1024,256]{1,0:T(8,128)}, u32[]{:S(2)}) copy-start(f32[1024,256]{1,0:T(8,128)} %get-tuple-element.9) | copy-start | bytes 3145732
  49.6 4.4 %copy-start.15 = (f32[512,256]{1,0:T(8,128)S(1)}, f32[512,256]{1,0:T(8,128)}, u32[]{:S(2)}) copy-start(f32[512,256]{1,0:T(8,128)} %gather_fusion.3) | copy-start | bytes 1572868
  56.8 4.7 %copy-start.9 = (f32[1024,256]{1,0:T(8,128)S(1)}, f32[1024,256]{1,0:T(8,128)}, u32[]{:S(2)}) copy-start(f32[1024,256]{1,0:T(8,128)} %gather_fusion.5) | copy-start | bytes 3145732
  61.5 1.9 %copy-start.12 = (f32[1024,256]{1,0:T(8,128)S(1)}, f32[1024,256]{1,0:T(8,128)}, u32[]{:S(2)}) copy-start(f32[1024,256]{1,0:T(8,128)} %gather_fusion.6) | copy-start | bytes 3145732
  63.3 4.4 %copy-start.13 = (f32[8,128,256]{2,1,0:T(8,128)}, f32[8,128,256]{2,1,0:T(8,128)S(1)}, u32[]{:S(2)}) copy-start(f32[8,128,256]{2,1,0:T(8,128)S(1)} %get-tuple-element.7) | copy-start | bytes 3145732
  63.3 1.6 copy-start.10
  63.4 1.9 %copy-start.11 = (f32[1024,256]{1,0:T(8,128)S(1)}, f32[1024,256]{1,0:T(8,128)}, u32[]{:S(2)}) copy-start(f32[1024,256]{1,0:T(8,128)} %gather_fusion.4) | copy-start | bytes 3145732
  65.3 2.5 %copy-start.16 = (f32[8,128,128]{2,1,0:T(8,128)}, f32[8,128,128]{2,1,0:T(8,128)S(1)}, u32[]{:S(2)}) copy-start(f32[8,128,128]{2,1,0:T(8,128)S(1)} %fusion.5) | copy-start | bytes 1572868
  65.3 2.5 %copy-start.8 = (f32[1024,256]{1,0:T(8,128)S(1)}, f32[1024,256]{1,0:T(8,128)}, u32[]{:S(2)}) copy-start(f32[1024,256]{1,0:T(8,128)} %get-tuple-element.9) | copy-start | bytes 3145732
  88.6 0.8 copy-start.4
  89.4 4.3 %copy-start.14 = (f32[8,128,256]{2,1,0:T(8,128)S(1)}, f32[8,128,256]{2,1,0:T(8,128)}, u32[]{:S(2)}) copy-start(f32[8,128,256]{2,1,0:T(8,128)} %copy-done.13) | copy-start | bytes 3145732
  89.4 54.8 %reduce-scatter.5.cloned.1.call-start = ((), (), s32[]{:S(2)}) async-start(), calls=%async_computation.3 | async-start | bytes 327680 | tf_op jit(solution)/shard_map/reduce_scatter | solution.py:101
  96.8 7.5 %copy-start.21 = (u32[32]{0:T(128)S(1)}, u32[32]{0:T(128)}, u32[]{:S(2)}) copy-start(u32[32]{0:T(128)} %constant.61) | copy-start | bytes 388
  96.8 8.8 %copy-start.18 = (s32[1,1,1,8,128]{4,3,2,1,0:T(8,128)S(1)}, s32[1,1,1,8,128]{4,3,2,1,0:T(8,128)}, u32[]{:S(2)}) copy-start(s32[1,1,1,8,128]{4,3,2,1,0:T(8,128)} %param.20) | copy-start | bytes 12292
  96.8 8.8 %copy-start.6 = (f32[1024,256]{1,0:T(8,128)S(1)}, f32[1024,256]{1,0:T(8,128)}, u32[]{:S(2)}) copy-start(f32[1024,256]{1,0:T(8,128)} %copy-done.5) | copy-start | bytes 3145732
  103.5 0.7 copy-start.1
  104.3 42.6 %reduce-scatter.3.cloned.1.call-start = ((), (), s32[]{:S(2)}) async-start(), calls=%async_computation.2 | async-start | bytes 327680 | tf_op jit(solution)/shard_map/reduce_scatter | solution.py:100
  112.8 30.9 %copy-start.19 = (f32[512]{0:T(512)S(1)}, f32[512]{0:T(512)}, u32[]{:S(2)}) copy-start(f32[512]{0:T(512)} %param.15) | copy-start | bytes 6148
  119.5 0.7 copy-start.3
  119.5 30.8 %copy-start.20 = (f32[256]{0:T(256)S(1)}, f32[256]{0:T(256)}, u32[]{:S(2)}) copy-start(f32[256]{0:T(256)} %param.13) | copy-start | bytes 3076
  144.2 5.1 %collective-permute-start.1 = (f32[64,256]{1,0:T(8,128)}, f32[64,256]{1,0:T(8,128)S(1)}, u32[]{:S(2)}, u32[]{:S(2)}) collective-permute-start(f32[64,256]{1,0:T(8,128)} %reduce-scatter.5.cloned.1.call-done), channel_id=1, source_target_pairs={{0,4},{4,8},{8,12},{12,0},{1,5},{5,9},{9,13},{13,1},{2,6},{6,10},{... | collective-permute-start | bytes 196616 | tf_op jit(solution)/shard_map/ppermute | solution.py:15
Sparse Core Ops, SparseCore 0:
  89.5 52.8 all-reduce.2
Sparse Core Ops, SparseCore 1:
  104.4 18.2 reduce-scatter.4
  125.7 20.0 reduce-scatter.2
where the time goes:
time: 176 us; the launch traced here: 175 us
  other arithmetic  63.1 us (36%)
  local copies, waits for them, and re-layouts  33 us (19%)
  waiting for transfers between devices  24.8 us (14%)
  matrix products  17.1 us (10%)
  between operations  16.5 us (9%)
  blocking collectives  15.6 us (9%)
  starting transfers between devices  5 us (3%)
    psum x1, waiting for transfers between devices, body(): rel_total = lax.psum(grel, ('bucket', 'sub'))  22.2 us
    scatter-add x2, other arithmetic, body(): gdst = gdst.at[d_ids].add(ddst).at[n_ids].add(dneg)  10.9 us
    unnamed x1, blocking collectives  9.14 us
    scatter-add x1, other arithmetic, body(): grel = grel.at[r_ids].add(dq * src_rows)  7.37 us
    scatter-add x1, other arithmetic, body(): gsrc = gsrc.at[s_ids].add(dq * rel_rows)  7.15 us
    scatter-add x1, other arithmetic, body(): grel.at[o_rel.reshape(-1)].add((dq_spill * src_rows).reshape(-1, width))  6.76 us
    scatter-add x1, other arithmetic, body(): gdst = gdst.at[o_dst.reshape(-1)].add(dd_spill.reshape(-1, width))  6.74 us
    scatter-add x1, other arithmetic, body(): gsrc.at[o_src.reshape(-1)].add((dq_spill * rel_rows).reshape(-1, width))  6.67 us
  transfers between devices with their start and end apart: 5, of which 2 were waited for; matrix products, arithmetic and copies ran while one was open for 33% of the time, Pallas kernels for 0%

commit v1 on v0

v1 whole, which is shorter than its diff:
```python
import functools

import jax
import jax.numpy as jnp
from jax import lax
from jax.experimental import pallas as pl
from jax.experimental.pallas import tpu as pltpu
from jax.sharding import PartitionSpec as P

F32 = jnp.float32
BF16 = jnp.bfloat16
LANES = 128
CHUNK = 256


def mm(a, b):
    return jnp.dot(a, b, preferred_element_type=F32)


def mm_nt(a, b):
    return lax.dot_general(a, b, (((1,), (1,)), ((), ())), preferred_element_type=F32)


def split(x):
    hi = x.astype(BF16)
    return hi, (x - hi.astype(F32)).astype(BF16)


def to_column(row, eye):
    return jnp.sum(jnp.where(eye, row, 0.0), axis=1, keepdims=True)


def to_row(column, eye):
    return jnp.sum(jnp.where(eye, column, 0.0), axis=0, keepdims=True)


def remote(src, dst, send, recv, **target):
    return pltpu.make_async_remote_copy(
        src_ref=src,
        dst_ref=dst,
        send_sem=send,
        recv_sem=recv,
        device_id=target,
        device_id_type=pl.DeviceIdType.MESH,
    )


def kernel(
    sizes,
    ent, ent_acc, rel, rel_acc, e_src, e_dst, e_rel, neg, o_src, o_dst, o_rel, count,
    new_ent, new_ent_acc, new_rel, new_rel_acc,
    neg_in, dst_tab, rel_core, rel_in, rel_all, ent_core, ent_in, moved_in, ent_all,
    ids, weight, src_hl, rel_hl, dst_hl, s_rows, r_rows, q_hi, q_lo, d_hot, s_hot, r_hot,
    xr_hi, xr_lo, xs_hi, xs_lo, gt_hi, gt_lo, g_rel, g_ent, share,
    s_neg, r_neg, s_tab, r_tab, s_rc, r_rc, s_rz, r_rz, s_ra, r_ra, s_rf, r_rf,
    s_ec, r_ec, s_ex, r_ex, s_mv, r_mv, s_ea, r_ea, s_ef, r_ef,
):
    n_bucket, n_rel, n_sub = sizes
    me_b = lax.axis_index("bucket")
    me_g = lax.axis_index("rel")
    me_s = lax.axis_index("sub")
    other = 1 - me_s
    ent_rows, width = ent.shape
    rel_rows = rel.shape[0]
    half_e, half_r = ent_rows // n_sub, rel_rows // n_sub
    own_e, own_r = half_e // n_rel, half_r // n_bucket
    spill = o_src.shape[0]
    block = e_src.shape[0] // n_sub
    tiles = block + spill
    edges = tiles * LANES

    def around(me, step, n):
        return lax.rem(me + step, n)

    barrier = pltpu.get_barrier_semaphore()
    for k in range(1, n_bucket):
        pl.semaphore_signal(barrier, inc=1, device_id={"bucket": around(me_b, k, n_bucket)},
                            device_id_type=pl.DeviceIdType.MESH)
    for k in range(1, n_rel):
        pl.semaphore_signal(barrier, inc=1, device_id={"rel": around(me_g, k, n_rel)},
                            device_id_type=pl.DeviceIdType.MESH)
    pl.semaphore_signal(barrier, inc=1, device_id={"sub": other},
                        device_id_type=pl.DeviceIdType.MESH)
    pl.semaphore_wait(barrier, n_bucket - 1 + n_rel - 1 + 1)

    my_half = pl.ds(pl.multiple_of(me_s * half_e, half_e), half_e)
    tab = remote(ent.at[my_half], dst_tab.at[my_half], s_tab.at[0], r_tab.at[0],
                 bucket=around(me_b, n_bucket - 1, n_bucket))
    tab.start()
    negs = remote(neg, neg_in, s_neg, r_neg, sub=other)
    negs.start()

    eye = (lax.broadcasted_iota(jnp.int32, (LANES, LANES), 0)
           == lax.broadcasted_iota(jnp.int32, (LANES, LANES), 1))
    lane_e = lax.broadcasted_iota(jnp.int32, (LANES, ent_rows), 1).astype(F32)
    lane_r = lax.broadcasted_iota(jnp.int32, (LANES, rel_rows), 1).astype(F32)
    sub_e = lax.broadcasted_iota(jnp.int32, (ent_rows, LANES), 0)
    sub_r = lax.broadcasted_iota(jnp.int32, (rel_rows, LANES), 0)

    for place, (mine, over) in enumerate(((e_src, o_src), (e_dst, o_dst), (e_rel, o_rel))):
        for t in range(block):
            ids[place, t] = mine[pl.ds(me_s * block + t, 1), :]
        for t in range(spill):
            ids[place, block + t] = over[pl.ds(t, 1), :]

    src_hl[0], src_hl[1] = split(ent[...])
    rel_hl[0], rel_hl[1] = split(rel[...])
    own = jnp.sum(jnp.where(lax.broadcasted_iota(jnp.int32, count.shape, 1) == me_b, count[...], 0)
                  .astype(F32), axis=1, keepdims=True)

    def gather(t, carry):
        rows = pl.ds(pl.multiple_of(t * LANES, LANES), LANES)
        s_id, d_id, r_id = ids[0, t], ids[1, t], ids[2, t]
        hot = (lane_e == to_column(s_id.astype(F32), eye)).astype(F32).astype(BF16)
        s = mm(hot, src_hl[0]) + mm(hot, src_hl[1])
        hot = (lane_r == to_column(r_id.astype(F32), eye)).astype(F32).astype(BF16)
        r = mm(hot, rel_hl[0]) + mm(hot, rel_hl[1])
        s_rows[rows] = s
        r_rows[rows] = r
        q_hi[rows], q_lo[rows] = split(s * r)
        hot = (lane_e == to_column(d_id.astype(F32), eye)).astype(F32)
        d_hot[rows] = hot
        live = ((t - block).astype(F32) < own).astype(F32)
        weight[t] = jnp.sum(hot, axis=0, keepdims=True) * (live * (1.0 / LANES))
        s_hot[:, rows] = (sub_e == s_id).astype(F32).astype(BF16)
        r_hot[:, rows] = (sub_r == r_id).astype(F32).astype(BF16)
        return carry

    lax.fori_loop(0, tiles, gather, 0)

    negs.wait_recv()
    times = jnp.zeros((1, ent_rows), F32)
    for held in (neg, neg_in):
        for t in range(held.shape[0]):
            column = to_column(held[pl.ds(t, 1), :].astype(F32), eye)
            times += jnp.sum((lane_e == column).astype(F32), axis=0, keepdims=True)
    n_neg = n_sub * neg.shape[0] * LANES
    for t in range(block):
        weight[t] = times * (1.0 / n_neg)

    tab.wait_recv()
    tab_core = remote(dst_tab.at[my_half], dst_tab.at[my_half], s_tab.at[1], r_tab.at[1], sub=other)
    tab_core.start()
    tab_core.wait_recv()
    dst_hl[0], dst_hl[1] = split(dst_tab[...])

    def score(c, carry):
        rows = pl.ds(pl.multiple_of(c * CHUNK, CHUNK), CHUNK)
        q_h, q_l = q_hi[rows], q_lo[rows]
        s = mm_nt(q_h, dst_hl[0]) + mm_nt(q_h, dst_hl[1]) + mm_nt(q_l, dst_hl[0])
        sig = lax.logistic(s)
        per = CHUNK // LANES
        w = jnp.concatenate(
            [jnp.broadcast_to(weight[c * per + i], (LANES, ent_rows)) for i in range(per)], axis=0)
        live = jnp.concatenate(
            [jnp.broadcast_to(((c * per + i - block).astype(F32) < own).astype(F32), (LANES, 1))
             for i in range(per)], axis=0)
        g = sig * w + d_hot[rows] * live * (sig - 1.0)
        g_h, g_l = split(g)
        dq = mm(g_h, dst_hl[0]) + mm(g_h, dst_hl[1]) + mm(g_l, dst_hl[0])
        xr_hi[rows], xr_lo[rows] = split(dq * s_rows[rows])
        xs_hi[rows], xs_lo[rows] = split(dq * r_rows[rows])
        gt_hi[:, rows], gt_lo[:, rows] = split(g.T)
        return carry

    lax.fori_loop(0, edges // CHUNK, score, 0)

    g_rel[...] = mm(r_hot[...], xr_hi[...]) + mm(r_hot[...], xr_lo[...])
    mine_r = pl.ds(pl.multiple_of(me_s * half_r, half_r), half_r)
    twin_r = pl.ds(pl.multiple_of(other * half_r, half_r), half_r)
    rel_c = remote(g_rel.at[twin_r], rel_core, s_rc, r_rc, sub=other)
    rel_c.start()

    g_ent[1] = mm(gt_hi[...], q_hi[...]) + mm(gt_hi[...], q_lo[...]) + mm(gt_lo[...], q_hi[...])
    twin_e = pl.ds(pl.multiple_of(other * half_e, half_e), half_e)

    def to_twin(which):
        copy = remote(g_ent.at[which, twin_e], ent_core.at[which], s_ec.at[which], r_ec.at[which],
                      sub=other)
        copy.start()
        return copy

    def to_rel(which):
        copies = []
        for k in range(1, n_rel):
            peer = around(me_g, k, n_rel)
            there = pl.ds(pl.multiple_of(peer * own_e, own_e), own_e)
            copy = remote(ent_core.at[which, there], ent_in.at[which, k], s_ex.at[which, k],
                          r_ex.at[which, k], rel=peer)
            copy.start()
            copies.append(copy)
        return copies

    here_e = pl.ds(pl.multiple_of(me_g * own_e, own_e), own_e)

    def summed(which, copies):
        total = ent_core[which, here_e]
        for k, copy in enumerate(copies):
            copy.wait_recv()
            total = total + ent_in[which, k + 1]
        return total

    dst_c = to_twin(1)

    rel_c.wait_recv()
    rel_core[...] = rel_core[...] + g_rel[mine_r]
    rel_z = []
    for k in range(1, n_bucket):
        peer = around(me_b, k, n_bucket)
        there = pl.ds(pl.multiple_of(peer * own_r, own_r), own_r)
        copy = remote(rel_core.at[there], rel_in.at[k], s_rz.at[k], r_rz.at[k], bucket=peer)
        copy.start()
        rel_z.append(copy)

    dst_c.wait_recv()
    ent_core[1] = ent_core[1] + g_ent[1, my_half]
    dst_x = to_rel(1)

    g_ent[0] = mm(s_hot[...], xs_hi[...]) + mm(s_hot[...], xs_lo[...])
    src_c = to_twin(0)

    share[...] = summed(1, dst_x)
    moved = remote(share, moved_in, s_mv, r_mv, bucket=around(me_b, 1, n_bucket))
    moved.start()

    src_c.wait_recv()
    ent_core[0] = ent_core[0] + g_ent[0, my_half]
    src_x = to_rel(0)

    total = rel_core[pl.ds(pl.multiple_of(me_b * own_r, own_r), own_r)]
    for k, copy in enumerate(rel_z):
        copy.wait_recv()
        total = total + rel_in[k + 1]

    def rows_r(owner):
        return pl.ds(pl.multiple_of(me_s * half_r + owner * own_r, own_r), own_r)

    rel_all[rows_r(me_b)] = total
    rel_a, rel_f = [], []
    for k in range(1, n_bucket):
        peer = around(me_b, k, n_bucket)
        copy = remote(rel_all.at[rows_r(me_b)], rel_all.at[rows_r(me_b)], s_ra.at[k], r_ra.at[k],
                      bucket=peer)
        copy.start()
        rel_a.append(copy)

    def forward_r(k):
        there = rows_r(around(me_b, n_bucket - k, n_bucket))
        copy = remote(rel_all.at[there], rel_all.at[there], s_rf.at[k], r_rf.at[k], sub=other)
        copy.start()
        rel_f.append(copy)

    forward_r(0)

    def rows_e(owner):
        return pl.ds(pl.multiple_of(me_s * half_e + owner * own_e, own_e), own_e)

    total = summed(0, src_x)
    moved.wait_recv()
    ent_all[rows_e(me_g)] = total + moved_in[...]
    ent_a, ent_f = [], []
    for k in range(1, n_rel):
        peer = around(me_g, k, n_rel)
        copy = remote(ent_all.at[rows_e(me_g)], ent_all.at[rows_e(me_g)], s_ea.at[k], r_ea.at[k],
                      rel=peer)
        copy.start()
        ent_a.append(copy)

    def forward_e(k):
        there = rows_e(around(me_g, n_rel - k, n_rel))
        copy = remote(ent_all.at[there], ent_all.at[there], s_ef.at[k], r_ef.at[k], sub=other)
        copy.start()
        ent_f.append(copy)

    forward_e(0)
    for k in range(1, n_rel):
        ent_a[k - 1].wait_recv()
        forward_e(k)

    def adagrad(table, accum, grads, out, out_acc, t):
        rows = pl.ds(t * LANES, LANES)
        grad = grads[rows]
        fresh = (to_column(accum[pl.ds(t, 1), :], eye)
                 + jnp.sum(grad * grad, axis=1, keepdims=True) * (1.0 / width))
        out[rows] = table[rows] - grad * (0.1 * lax.rsqrt(fresh))
        out_acc[pl.ds(t, 1), :] = to_row(fresh, eye)

    for copy in ent_f:
        copy.wait_recv()
    for t in range(ent_rows // LANES):
        adagrad(ent, ent_acc, ent_all, new_ent, new_ent_acc, t)

    for k in range(1, n_bucket):
        rel_a[k - 1].wait_recv()
        forward_r(k)
    for copy in rel_f:
        copy.wait_recv()
    for t in range(rel_rows // LANES):
        adagrad(rel, rel_acc, rel_all, new_rel, new_rel_acc, t)

    for copy in [tab, negs, tab_core, rel_c, dst_c, src_c, moved] + (
            rel_z + dst_x + src_x + rel_a + rel_f + ent_a + ent_f):
        copy.wait_send()


def body(sizes, entity, entity_acc, relation, relation_acc, edge_src, edge_dst, edge_rel, negatives,
         ovf_src, ovf_dst, ovf_rel, ovf_count):
    n_bucket, n_rel, n_sub = sizes
    ent_rows, width = entity.shape
    rel_rows = relation.shape[0]
    lined = lambda x: x.reshape(-1, LANES)
    half_e, half_r = ent_rows // n_sub, rel_rows // n_sub
    own_e, own_r = half_e // n_rel, half_r // n_bucket
    tiles = edge_src.size // n_sub // LANES + ovf_src.size // LANES
    edges = tiles * LANES
    neg_rows = negatives.size // LANES
    vmem = pltpu.VMEM
    dma = pltpu.SemaphoreType.DMA
    scratch = [
        vmem((neg_rows, LANES), jnp.int32),
        vmem((ent_rows, width), F32),
        vmem((half_r, width), F32),
        vmem((n_bucket, own_r, width), F32),
        vmem((rel_rows, width), F32),
        vmem((2, half_e, width), F32),
        vmem((2, n_rel, own_e, width), F32),
        vmem((own_e, width), F32),
        vmem((ent_rows, width), F32),
        vmem((3, tiles, 1, LANES), jnp.int32),
        vmem((tiles, 1, ent_rows), F32),
        vmem((2, ent_rows, width), BF16),
        vmem((2, rel_rows, width), BF16),
        vmem((2, ent_rows, width), BF16),
        vmem((edges, width), F32),
        vmem((edges, width), F32),
        vmem((edges, width), BF16),
        vmem((edges, width), BF16),
        vmem((edges, ent_rows), F32),
        vmem((ent_rows, edges), BF16),
        vmem((rel_rows, edges), BF16),
        vmem((edges, width), BF16),
        vmem((edges, width), BF16),
        vmem((edges, width), BF16),
        vmem((edges, width), BF16),
        vmem((ent_rows, edges), BF16),
        vmem((ent_rows, edges), BF16),
        vmem((rel_rows, width), F32),
        vmem((2, ent_rows, width), F32),
        vmem((own_e, width), F32),
        dma, dma,
        dma((2,)), dma((2,)),
        dma, dma,
        dma((n_bucket,)), dma((n_bucket,)),
        dma((n_bucket,)), dma((n_bucket,)),
        dma((n_bucket,)), dma((n_bucket,)),
        dma((2,)), dma((2,)),
        dma((2, n_rel)), dma((2, n_rel)),
        dma, dma,
        dma((n_rel,)), dma((n_rel,)),
        dma((n_rel,)), dma((n_rel,)),
    ]
    new_ent, new_ent_acc, new_rel, new_rel_acc = pl.pallas_call(
        functools.partial(kernel, sizes),
        out_shape=(
            jax.ShapeDtypeStruct(entity.shape, F32),
            jax.ShapeDtypeStruct((ent_rows // LANES, LANES), F32),
            jax.ShapeDtypeStruct(relation.shape, F32),
            jax.ShapeDtypeStruct((rel_rows // LANES, LANES), F32),
        ),
        in_specs=[pl.BlockSpec(memory_space=vmem)] * 12,
        out_specs=[pl.BlockSpec(memory_space=vmem)] * 4,
        scratch_shapes=scratch,
        compiler_params=pltpu.CompilerParams(
            collective_id=0, has_side_effects=True, vmem_limit_bytes=40 * 1024 * 1024),
    )(
        entity, lined(entity_acc), relation, lined(relation_acc),
        lined(edge_src), lined(edge_dst), lined(edge_rel), lined(negatives),
        lined(ovf_src), lined(ovf_dst), lined(ovf_rel), ovf_count.reshape(1, -1),
    )
    return new_ent, new_ent_acc.reshape(-1), new_rel, new_rel_acc.reshape(-1)


def solution(mesh):
    sizes = (mesh.shape["bucket"], mesh.shape["rel"], mesh.shape["sub"])
    edge = P(("groups", "bucket"), "rel", None, None)
    over = P(("groups", "bucket"), "rel", "sub", None, None)
    rows = (
        P(("groups", "bucket"), None),
        P(("groups", "bucket")),
        P(("groups", "rel"), None),
        P(("groups", "rel")),
    )
    return jax.shard_map(
        functools.partial(body, sizes),
        mesh=mesh,
        in_specs=rows + (edge, edge, edge, P(("groups", "bucket"), "rel", None, "sub"),
                         over, over, over, P(("groups", "rel"), "sub", None)),
        out_specs=rows,
        check_vma=False,
    )
```

time: 176 us -> 42.9 us (0.24)
  other arithmetic: 63.1 us -> 0 us
  Pallas kernels: 0 us -> 33.8 us
  local copies, waits for them, and re-layouts: 33 us -> 8.07 us
  waiting for transfers between devices: 24.8 us -> 0 us
  matrix products: 17.1 us -> 0 us
  between operations: 16.5 us -> 0.7 us
  blocking collectives: 15.6 us -> 0 us
  starting transfers between devices: 5 us -> 0 us
    scatter-add x7 -> x0, other arithmetic: 45.5 us -> none  [the longest x2 10.9 us: body(): gdst = gdst.at[d_ids].add(ddst).at[n_ids].add(dneg)]
    pallas_call x0 -> x1, Pallas kernels: none -> 33.8 us  [body(): pl.pallas_call(functools.partial(kernel, sizes), out_shape=(jax.ShapeDtyp...]
    gather x7 -> x0, local copies, waits for them, and re-layouts: 28.8 us -> none  [the longest x1 5.67 us: body(): src_rows = entity[s_ids]]
    psum x1 -> x0, waiting for transfers between devices: 22.2 us -> none  [body(): rel_total = lax.psum(grel, ('bucket', 'sub'))]
    dot_general x6 -> x0, matrix products: 17.1 us -> none  [the longest x1 4.36 us: block_grads(): dnegrows = lax.dot_general(dneg, q, (((0,), (0,)), ((), ())), precision=HI)]
    unnamed x1 -> x0, blocking collectives: 9.14 us -> none
    reduce_sum x5 -> x0, other arithmetic: 7.66 us -> none  [the longest x1 2.38 us: block_grads(): pos = jnp.sum(q * dst_rows, axis=-1)]
    all_gather x1 -> x0, blocking collectives: 6.47 us -> none  [body(): lax.all_gather(part_rows, ('rel', 'sub'), axis=0, tiled=True)]
  transfers between devices with their start and end apart: 5 -> 0, of which waited for: 2 -> 0; matrix products, arithmetic and copies ran while one was open for 33% -> 0% of each run, Pallas kernels for 0% -> 0%
where the time goes in v1:
time: 42.9 us; the launch traced here: 42.6 us
  Pallas kernels  33.8 us (79%)
  local copies, waits for them, and re-layouts  8.07 us (19%)
  between operations  0.7 us (2%)
    pallas_call x1, Pallas kernels, body(): pl.pallas_call(functools.partial(kernel, sizes), out_shape=(jax.ShapeDtyp...  33.8 us
    unnamed x28, local copies, waits for them, and re-layouts  8.07 us

profile of v1, /device:TPU:1, one launch (start us, length us, event | category | flops | bytes accessed | tf_op | source)
XLA Modules:
  0.0 42.6 jit_solution(12400828015043276514)
XLA Ops:
  0.6 0.0 copy-start.8
  0.6 0.0 copy-start.5
  0.7 0.0 copy-start.4
  0.7 0.0 copy-start.3
  0.7 0.0 copy-start.2
  0.7 0.0 copy-start.11
  0.7 0.6 %copy-done.8 = f32[512]{0:T(512)S(1)} copy-done((f32[512]{0:T(512)S(1)}, f32[512]{0:T(512)}, u32[]{:S(2)}) %copy-start.8) | copy-done | bytes 2072
  1.3 0.0 copy-done.5
  1.3 0.0 copy-done.4
  1.4 0.0 copy-done.3
  1.4 0.0 copy-done.2
  1.4 0.0 copy-done.11
  1.4 0.0 copy-start
  1.4 1.0 %copy-done = f32[512,256]{1,0:T(8,128)S(1)} copy-done((f32[512,256]{1,0:T(8,128)S(1)}, f32[512,256]{1,0:T(8,128)}, u32[]{:S(2)}) %copy-start) | copy-done | bytes 524312
  2.4 0.0 copy-start.1
  2.4 0.9 %copy-done.1 = f32[256,256]{1,0:T(8,128)S(1)} copy-done((f32[256,256]{1,0:T(8,128)S(1)}, f32[256,256]{1,0:T(8,128)}, u32[]{:S(2)}) %copy-start.1) | copy-done | bytes 262168
  3.4 0.0 copy-start.6
  3.4 0.7 %copy-done.6 = s32[1,1,1,8,128]{4,3,2,1,0:T(8,128)S(1)} copy-done((s32[1,1,1,8,128]{4,3,2,1,0:T(8,128)S(1)}, s32[1,1,1,8,128]{4,3,2,1,0:T(8,128)}, u32[]{:S(2)}) %copy-start.6) | copy-done | bytes 4120
  4.1 0.0 copy-start.7
  4.1 0.7 %copy-done.7 = s32[1,1,1,8,128]{4,3,2,1,0:T(8,128)S(1)} copy-done((s32[1,1,1,8,128]{4,3,2,1,0:T(8,128)S(1)}, s32[1,1,1,8,128]{4,3,2,1,0:T(8,128)}, u32[]{:S(2)}) %copy-start.7) | copy-done | bytes 4120
  4.8 0.0 copy-start.9
  4.8 0.7 %copy-done.9 = s32[1,1,1,512]{3,2,1,0:T(1,128)S(1)} copy-done((s32[1,1,1,512]{3,2,1,0:T(1,128)S(1)}, s32[1,1,1,512]{3,2,1,0:T(1,128)}, u32[]{:S(2)}) %copy-start.9) | copy-done | bytes 2072
  5.4 0.0 copy-start.10
  5.4 0.7 %copy-done.10 = f32[256]{0:T(256)S(1)} copy-done((f32[256]{0:T(256)S(1)}, f32[256]{0:T(256)}, u32[]{:S(2)}) %copy-start.10) | copy-done | bytes 1048
  6.1 33.8 %shard_map.147 = (f32[256,256]{1,0:T(8,128)S(1)}, f32[2,128]{1,0:T(2,128)S(1)}, f32[512,256]{1,0:T(8,128)S(1)}, f32[4,128]{1,0:T(4,128)S(1)}) custom-call(f32[256,256]{1,0:T(8,128)S(1)} %copy-done.1, f32[2,128]{1,0:T(2,128)S(1)} %bitcast.21, f32[512,256]{1,0:T(8,128)S(1)} %copy-done, f32[4,128]{1,0:T(4,128)S(1)} %bitcast.18, s32[8,128]{1,0:T(8,128)S(1)} %bitcast.12, ...), custom_call_target="tpu_custom_call" | custom-call | tf_op jit(solution)/shard_map/pallas_call | solution.py:362
  39.9 0.7 %copy.20 = f32[256,256]{1,0:T(8,128)} copy(f32[256,256]{1,0:T(8,128)S(1)} %get-tuple-element.16) | data formatting | bytes 524288
  40.6 0.6 %copy.21 = f32[256]{0:T(256)} copy(f32[256]{0:T(256)S(1)} %bitcast.22) | data formatting | bytes 2048
  41.2 0.8 %copy.22 = f32[512,256]{1,0:T(8,128)} copy(f32[512,256]{1,0:T(8,128)S(1)} %get-tuple-element.18) | data formatting | bytes 1048576
  42.0 0.6 %copy.23 = f32[512]{0:T(512)} copy(f32[512]{0:T(512)S(1)} %bitcast.20) | data formatting | bytes 4096
Async XLA Ops:
  0.6 0.7 %copy-start.8 = (f32[512]{0:T(512)S(1)}, f32[512]{0:T(512)}, u32[]{:S(2)}) copy-start(f32[512]{0:T(512)} %param.15) | copy-start | bytes 6148
  0.6 0.7 %copy-start.5 = (s32[1,1,1,8,128]{4,3,2,1,0:T(8,128)S(1)}, s32[1,1,1,8,128]{4,3,2,1,0:T(8,128)}, u32[]{:S(2)}) copy-start(s32[1,1,1,8,128]{4,3,2,1,0:T(8,128)} %param.20) | copy-start | bytes 12292
  0.7 0.7 %copy-start.4 = (s32[1,1,1,1024]{3,2,1,0:T(1,128)S(1)}, s32[1,1,1,1024]{3,2,1,0:T(1,128)}, u32[]{:S(2)}) copy-start(s32[1,1,1,1024]{3,2,1,0:T(1,128)} %param.18) | copy-start | bytes 12292
  0.7 0.7 %copy-start.3 = (s32[1,1,1,1024]{3,2,1,0:T(1,128)S(1)}, s32[1,1,1,1024]{3,2,1,0:T(1,128)}, u32[]{:S(2)}) copy-start(s32[1,1,1,1024]{3,2,1,0:T(1,128)} %param.17) | copy-start | bytes 12292
  0.7 0.7 %copy-start.2 = (s32[1,1,1,1024]{3,2,1,0:T(1,128)S(1)}, s32[1,1,1,1024]{3,2,1,0:T(1,128)}, u32[]{:S(2)}) copy-start(s32[1,1,1,1024]{3,2,1,0:T(1,128)} %param.16) | copy-start | bytes 12292
  0.7 0.7 %copy-start.11 = (s32[1,1,4]{2,1,0:T(1,128)S(1)}, s32[1,1,4]{2,1,0:T(1,128)}, u32[]{:S(2)}) copy-start(s32[1,1,4]{2,1,0:T(1,128)} %param.23) | copy-start | bytes 52
  1.4 1.0 %copy-start = (f32[512,256]{1,0:T(8,128)S(1)}, f32[512,256]{1,0:T(8,128)}, u32[]{:S(2)}) copy-start(f32[512,256]{1,0:T(8,128)} %rel.1) | copy-start | bytes 1572868
  2.4 0.9 %copy-start.1 = (f32[256,256]{1,0:T(8,128)S(1)}, f32[256,256]{1,0:T(8,128)}, u32[]{:S(2)}) copy-start(f32[256,256]{1,0:T(8,128)} %ent.1) | copy-start | bytes 786436
  3.4 0.7 %copy-start.6 = (s32[1,1,1,8,128]{4,3,2,1,0:T(8,128)S(1)}, s32[1,1,1,8,128]{4,3,2,1,0:T(8,128)}, u32[]{:S(2)}) copy-start(s32[1,1,1,8,128]{4,3,2,1,0:T(8,128)} %param.21) | copy-start | bytes 12292
  4.1 0.7 %copy-start.7 = (s32[1,1,1,8,128]{4,3,2,1,0:T(8,128)S(1)}, s32[1,1,1,8,128]{4,3,2,1,0:T(8,128)}, u32[]{:S(2)}) copy-start(s32[1,1,1,8,128]{4,3,2,1,0:T(8,128)} %param.22) | copy-start | bytes 12292
  4.8 0.7 %copy-start.9 = (s32[1,1,1,512]{3,2,1,0:T(1,128)S(1)}, s32[1,1,1,512]{3,2,1,0:T(1,128)}, u32[]{:S(2)}) copy-start(s32[1,1,1,512]{3,2,1,0:T(1,128)} %param.19) | copy-start | bytes 6148
  5.4 0.7 %copy-start.10 = (f32[256]{0:T(256)S(1)}, f32[256]{0:T(256)}, u32[]{:S(2)}) copy-start(f32[256]{0:T(256)} %param.13) | copy-start | bytes 3076

commit v2 on v1

--- a/solution.py
+++ b/solution.py
@@ -47,11 +47,13 @@
 
 def kernel(
     sizes,
-    ent, ent_acc, rel, rel_acc, e_src, e_dst, e_rel, neg, o_src, o_dst, o_rel, count,
-    new_ent, new_ent_acc, new_rel, new_rel_acc,
+    a_ent, a_ent_acc, a_rel, a_rel_acc, a_src, a_dst, a_typ, a_neg, a_o_src, a_o_dst, a_o_rel, a_count,
+    out_ent, out_ent_acc, out_rel, out_rel_acc,
+    ent, ent_acc, rel, rel_acc, e_src, e_dst, e_rel, neg, o_src, o_dst, o_rel, count, s_load,
     neg_in, dst_tab, rel_core, rel_in, rel_all, ent_core, ent_in, moved_in, ent_all,
     ids, weight, src_hl, rel_hl, dst_hl, s_rows, r_rows, q_hi, q_lo, d_hot, s_hot, r_hot,
-    xr_hi, xr_lo, xs_hi, xs_lo, gt_hi, gt_lo, g_rel, g_ent, share,
+    xr_hi, xr_lo, xs_hi, xs_lo, gt_hi, gt_lo, rel_out, rel_own, g_ent, share,
+    ent_new, ent_new_acc, rel_new, rel_new_acc, s_out,
     s_neg, r_neg, s_tab, r_tab, s_rc, r_rc, s_rz, r_rz, s_ra, r_ra, s_rf, r_rf,
     s_ec, r_ec, s_ex, r_ex, s_mv, r_mv, s_ea, r_ea, s_ef, r_ef,
 ):
@@ -72,6 +74,16 @@
     def around(me, step, n):
         return lax.rem(me + step, n)
 
+    loads = [
+        pltpu.make_async_copy(there, here, s_load.at[i])
+        for i, (there, here) in enumerate((
+            (a_src, e_src), (a_dst, e_dst), (a_typ, e_rel), (a_neg, neg), (a_o_src, o_src),
+            (a_o_dst, o_dst), (a_o_rel, o_rel), (a_count, count), (a_ent, ent), (a_rel, rel),
+            (a_ent_acc, ent_acc), (a_rel_acc, rel_acc)))
+    ]
+    for copy in loads:
+        copy.start()
+
     barrier = pltpu.get_barrier_semaphore()
     for k in range(1, n_bucket):
         pl.semaphore_signal(barrier, inc=1, device_id={"bucket": around(me_b, k, n_bucket)},
@@ -84,12 +96,14 @@
     pl.semaphore_wait(barrier, n_bucket - 1 + n_rel - 1 + 1)
 
     my_half = pl.ds(pl.multiple_of(me_s * half_e, half_e), half_e)
-    tab = remote(ent.at[my_half], dst_tab.at[my_half], s_tab.at[0], r_tab.at[0],
+    tab = remote(a_ent.at[my_half], dst_tab.at[my_half], s_tab.at[0], r_tab.at[0],
                  bucket=around(me_b, n_bucket - 1, n_bucket))
     tab.start()
-    negs = remote(neg, neg_in, s_neg, r_neg, sub=other)
+    negs = remote(a_neg, neg_in, s_neg, r_neg, sub=other)
     negs.start()
 
+    for copy in loads:
+        copy.wait()
     eye = (lax.broadcasted_iota(jnp.int32, (LANES, LANES), 0)
            == lax.broadcasted_iota(jnp.int32, (LANES, LANES), 1))
     lane_e = lax.broadcasted_iota(jnp.int32, (LANES, ent_rows), 1).astype(F32)
@@ -163,13 +177,58 @@
         gt_hi[:, rows], gt_lo[:, rows] = split(g.T)
         return carry
 
-    lax.fori_loop(0, edges // CHUNK, score, 0)
-
-    g_rel[...] = mm(r_hot[...], xr_hi[...]) + mm(r_hot[...], xr_lo[...])
-    mine_r = pl.ds(pl.multiple_of(me_s * half_r, half_r), half_r)
-    twin_r = pl.ds(pl.multiple_of(other * half_r, half_r), half_r)
-    rel_c = remote(g_rel.at[twin_r], rel_core, s_rc, r_rc, sub=other)
-    rel_c.start()
+    lax.fori_loop(0, edges // CHUNK, score, 0, unroll=True)
+
+    mine_r, twin_r = me_s * half_r, other * half_r
+    hop, cut = n_bucket // 2, own_r // 2
+
+    def part(base, k, half=None):
+        first = base + around(me_b, k % n_bucket, n_bucket) * own_r
+        if half is None:
+            return pl.ds(pl.multiple_of(first, own_r), own_r)
+        return pl.ds(pl.multiple_of(first + half * cut, cut), cut)
+
+    def scatter_r(base):
+        hot = r_hot[pl.ds(pl.multiple_of(base, half_r), half_r), :]
+        return mm(hot, xr_hi[...]) + mm(hot, xr_lo[...])
+
+    rel_out[...] = scatter_r(twin_r)
+    order = [hop] + [k * way for k in range(hop - 1, 0, -1) for way in (1, -1)] + [0]
+    rel_c = {}
+    for i, k in enumerate(order):
+        copy = remote(rel_out.at[part(0, k)], rel_core.at[part(0, k)], s_rc.at[i], r_rc.at[i],
+                      sub=other)
+        copy.start()
+        rel_c[k] = copy
+    rel_own[...] = scatter_r(mine_r)
+
+    def of_chip(k):
+        rel_c[k].wait_recv()
+        rel_core[part(0, k)] = rel_core[part(0, k)] + rel_own[part(0, k)]
+
+    def toward(way):
+        return around(me_b, 1 if way == 0 else n_bucket - 1, n_bucket)
+
+    rel_z = {}
+
+    def pass_on(way, half, t):
+        k = (hop - t) * (1 if way == 0 else -1)
+        rows = part(0, k, half)
+        if (way, half, t - 1) in rel_z:
+            rel_z[way, half, t - 1].wait_recv()
+            rel_core[rows] = rel_core[rows] + rel_in[way, half, t - 1]
+        copy = remote(rel_core.at[rows], rel_in.at[way, half, t], s_rz.at[way, half, t],
+                      r_rz.at[way, half, t], bucket=toward(way))
+        copy.start()
+        rel_z[way, half, t] = copy
+
+    of_chip(hop)
+    for way in range(2):
+        pass_on(way, way, 0)
+    if hop > 1:
+        for way, k in ((0, hop - 1), (1, 1 - hop)):
+            of_chip(k)
+            pass_on(way, 1 - way, 1)
 
     g_ent[1] = mm(gt_hi[...], q_hi[...]) + mm(gt_hi[...], q_lo[...]) + mm(gt_lo[...], q_hi[...])
     twin_e = pl.ds(pl.multiple_of(other * half_e, half_e), half_e)
@@ -202,55 +261,63 @@
 
     dst_c = to_twin(1)
 
-    rel_c.wait_recv()
-    rel_core[...] = rel_core[...] + g_rel[mine_r]
-    rel_z = []
-    for k in range(1, n_bucket):
-        peer = around(me_b, k, n_bucket)
-        there = pl.ds(pl.multiple_of(peer * own_r, own_r), own_r)
-        copy = remote(rel_core.at[there], rel_in.at[k], s_rz.at[k], r_rz.at[k], bucket=peer)
-        copy.start()
-        rel_z.append(copy)
+    if hop > 1:
+        for way in range(2):
+            pass_on(way, way, 1)
+
+    g_ent[0] = mm(s_hot[...], xs_hi[...]) + mm(s_hot[...], xs_lo[...])
+    src_c = to_twin(0)
 
     dst_c.wait_recv()
     ent_core[1] = ent_core[1] + g_ent[1, my_half]
     dst_x = to_rel(1)
 
-    g_ent[0] = mm(s_hot[...], xs_hi[...]) + mm(s_hot[...], xs_lo[...])
-    src_c = to_twin(0)
+    for t in range(2, hop):
+        for way, k in ((0, hop - t), (1, t - hop)):
+            of_chip(k)
+            for half in (way, 1 - way):
+                pass_on(way, half, t)
+    of_chip(0)
+
+    for half in range(2):
+        total = rel_core[part(0, 0, half)]
+        for way in range(2):
+            if (way, half, hop - 1) in rel_z:
+                rel_z[way, half, hop - 1].wait_recv()
+                total = total + rel_in[way, half, hop - 1]
+        rel_all[part(mine_r, 0, half)] = total
+    rel_a, rel_f = {}, []
+
+    def hand_on(way, t):
+        rows = part(mine_r, -t if way == 0 else t, way if t == hop - 1 else None)
+        copy = remote(rel_all.at[rows], rel_all.at[rows], s_ra.at[way, t], r_ra.at[way, t],
+                      bucket=toward(way))
+        copy.start()
+        rel_a[way, t] = copy
+
+    def forward_r(rows):
+        i = len(rel_f)
+        copy = remote(rel_all.at[rows], rel_all.at[rows], s_rf.at[i], r_rf.at[i], sub=other)
+        copy.start()
+        rel_f.append(copy)
+
+    for way in range(2):
+        hand_on(way, 0)
+    forward_r(part(mine_r, 0))
+
+    src_c.wait_recv()
+    ent_core[0] = ent_core[0] + g_ent[0, my_half]
+    src_x = to_rel(0)
 
     share[...] = summed(1, dst_x)
     moved = remote(share, moved_in, s_mv, r_mv, bucket=around(me_b, 1, n_bucket))
     moved.start()
 
-    src_c.wait_recv()
-    ent_core[0] = ent_core[0] + g_ent[0, my_half]
-    src_x = to_rel(0)
-
-    total = rel_core[pl.ds(pl.multiple_of(me_b * own_r, own_r), own_r)]
-    for k, copy in enumerate(rel_z):
-        copy.wait_recv()
-        total = total + rel_in[k + 1]
-
-    def rows_r(owner):
-        return pl.ds(pl.multiple_of(me_s * half_r + owner * own_r, own_r), own_r)
-
-    rel_all[rows_r(me_b)] = total
-    rel_a, rel_f = [], []
-    for k in range(1, n_bucket):
-        peer = around(me_b, k, n_bucket)
-        copy = remote(rel_all.at[rows_r(me_b)], rel_all.at[rows_r(me_b)], s_ra.at[k], r_ra.at[k],
-                      bucket=peer)
-        copy.start()
-        rel_a.append(copy)
-
-    def forward_r(k):
-        there = rows_r(around(me_b, n_bucket - k, n_bucket))
-        copy = remote(rel_all.at[there], rel_all.at[there], s_rf.at[k], r_rf.at[k], sub=other)
-        copy.start()
-        rel_f.append(copy)
-
-    forward_r(0)
+    for t in range(1, hop):
+        for way in range(2):
+            rel_a[way, t - 1].wait_recv()
+            hand_on(way, t)
+            forward_r(part(mine_r, -t if way == 0 else t))
 
     def rows_e(owner):
         return pl.ds(pl.multiple_of(me_s * half_e + owner * own_e, own_e), own_e)
@@ -273,34 +340,59 @@
         ent_f.append(copy)
 
     forward_e(0)
+
+    for way in range(2):
+        rel_a[way, hop - 1].wait_recv()
+        forward_r(part(mine_r, -hop if way == 0 else hop, way))
+
+    stores = []
+
+    def adagrad(table, accum, grads, staged, staged_acc, out, first, count, sem):
+        first = pl.multiple_of(first, count)
+        for i in range(count // LANES):
+            rows = pl.ds(pl.multiple_of(first + i * LANES, LANES), LANES)
+            at = pl.ds(first // LANES + i, 1)
+            grad = grads[rows]
+            fresh = (to_column(accum[at, :], eye)
+                     + jnp.sum(grad * grad, axis=1, keepdims=True) * (1.0 / width))
+            staged[rows] = table[rows] - grad * (0.1 * lax.rsqrt(fresh))
+            staged_acc[at, :] = to_row(fresh, eye)
+        whole = pl.ds(first, count)
+        copy = pltpu.make_async_copy(staged.at[whole], out.at[whole], s_out.at[sem])
+        copy.start()
+        stores.append(copy)
+
+    adagrad(rel, rel_acc, rel_all, rel_new, rel_new_acc, out_rel, mine_r, half_r, 0)
     for k in range(1, n_rel):
         ent_a[k - 1].wait_recv()
         forward_e(k)
-
-    def adagrad(table, accum, grads, out, out_acc, t):
-        rows = pl.ds(t * LANES, LANES)
-        grad = grads[rows]
-        fresh = (to_column(accum[pl.ds(t, 1), :], eye)
-                 + jnp.sum(grad * grad, axis=1, keepdims=True) * (1.0 / width))
-        out[rows] = table[rows] - grad * (0.1 * lax.rsqrt(fresh))
-        out_acc[pl.ds(t, 1), :] = to_row(fresh, eye)
-
+    adagrad(ent, ent_acc, ent_all, ent_new, ent_new_acc, out_ent, me_s * half_e, half_e, 1)
+    for copy in rel_f:
+        copy.wait_recv()
+    adagrad(rel, rel_acc, rel_all, rel_new, rel_new_acc, out_rel, twin_r, half_r, 2)
     for copy in ent_f:
         copy.wait_recv()
-    for t in range(ent_rows // LANES):
-        adagrad(ent, ent_acc, ent_all, new_ent, new_ent_acc, t)
-
-    for k in range(1, n_bucket):
-        rel_a[k - 1].wait_recv()
-        forward_r(k)
-    for copy in rel_f:
-        copy.wait_recv()
-    for t in range(rel_rows // LANES):
-        adagrad(rel, rel_acc, rel_all, new_rel, new_rel_acc, t)
-
-    for copy in [tab, negs, tab_core, rel_c, dst_c, src_c, moved] + (
-            rel_z + dst_x + src_x + rel_a + rel_f + ent_a + ent_f):
+    adagrad(ent, ent_acc, ent_all, ent_new, ent_new_acc, out_ent, other * half_e, half_e, 3)
+    for i, (here, there) in enumerate(((rel_new_acc, out_rel_acc), (ent_new_acc, out_ent_acc))):
+        copy = pltpu.make_async_copy(here, there, s_out.at[4 + i])
+        copy.start()
+        stores.append(copy)
+
+    for copy in [tab, negs, tab_core, dst_c, src_c, moved] + (
+            list(rel_c.values()) + list(rel_z.values()) + list(rel_a.values())
+            + dst_x + src_x + rel_f + ent_a + ent_f):
         copy.wait_send()
+    for copy in stores:
+        copy.wait()
+
+
+def store(*refs):
+    sems = refs[-1]
+    copies = [pltpu.make_async_copy(refs[i], refs[4 + i], sems.at[i]) for i in range(4)]
+    for copy in copies:
+        copy.start()
+    for copy in copies:
+        copy.wait()
 
 
 def body(sizes, entity, entity_acc, relation, relation_acc, edge_src, edge_dst, edge_rel, negatives,
@@ -314,13 +406,19 @@
     tiles = edge_src.size // n_sub // LANES + ovf_src.size // LANES
     edges = tiles * LANES
     neg_rows = negatives.size // LANES
+    hop = n_bucket // 2
     vmem = pltpu.VMEM
     dma = pltpu.SemaphoreType.DMA
-    scratch = [
+    args = (
+        entity, lined(entity_acc), relation, lined(relation_acc),
+        lined(edge_src), lined(edge_dst), lined(edge_rel), lined(negatives),
+        lined(ovf_src), lined(ovf_dst), lined(ovf_rel), ovf_count.reshape(1, -1),
+    )
+    scratch = [vmem(arg.shape, arg.dtype) for arg in args] + [dma((len(args),))] + [
         vmem((neg_rows, LANES), jnp.int32),
         vmem((ent_rows, width), F32),
         vmem((half_r, width), F32),
-        vmem((n_bucket, own_r, width), F32),
+        vmem((2, 2, hop, own_r // 2, width), F32),
         vmem((rel_rows, width), F32),
         vmem((2, half_e, width), F32),
         vmem((2, n_rel, own_e, width), F32),
@@ -344,39 +442,43 @@
         vmem((edges, width), BF16),
         vmem((ent_rows, edges), BF16),
         vmem((ent_rows, edges), BF16),
-        vmem((rel_rows, width), F32),
+        vmem((half_r, width), F32),
+        vmem((half_r, width), F32),
         vmem((2, ent_rows, width), F32),
         vmem((own_e, width), F32),
+        vmem(args[0].shape, F32), vmem(args[1].shape, F32),
+        vmem(args[2].shape, F32), vmem(args[3].shape, F32),
+        dma((6,)),
         dma, dma,
         dma((2,)), dma((2,)),
-        dma, dma,
         dma((n_bucket,)), dma((n_bucket,)),
-        dma((n_bucket,)), dma((n_bucket,)),
-        dma((n_bucket,)), dma((n_bucket,)),
+        dma((2, 2, hop)), dma((2, 2, hop)),
+        dma((2, hop)), dma((2, hop)),
+        dma((n_bucket + 1,)), dma((n_bucket + 1,)),
         dma((2,)), dma((2,)),
         dma((2, n_rel)), dma((2, n_rel)),
         dma, dma,
         dma((n_rel,)), dma((n_rel,)),
         dma((n_rel,)), dma((n_rel,)),
     ]
-    new_ent, new_ent_acc, new_rel, new_rel_acc = pl.pallas_call(
+    out_shape = tuple(jax.ShapeDtypeStruct(arg.shape, F32) for arg in args[:4])
+    made = pl.pallas_call(
         functools.partial(kernel, sizes),
-        out_shape=(
-            jax.ShapeDtypeStruct(entity.shape, F32),
-            jax.ShapeDtypeStruct((ent_rows // LANES, LANES), F32),
-            jax.ShapeDtypeStruct(relation.shape, F32),
-            jax.ShapeDtypeStruct((rel_rows // LANES, LANES), F32),
-        ),
-        in_specs=[pl.BlockSpec(memory_space=vmem)] * 12,
-        out_specs=[pl.BlockSpec(memory_space=vmem)] * 4,
+        out_shape=out_shape,
+        in_specs=[pl.BlockSpec(memory_space=pltpu.HBM)] * len(args),
+        out_specs=[pl.BlockSpec(memory_space=pltpu.HBM)] * 4,
         scratch_shapes=scratch,
         compiler_params=pltpu.CompilerParams(
-            collective_id=0, has_side_effects=True, vmem_limit_bytes=40 * 1024 * 1024),
-    )(
-        entity, lined(entity_acc), relation, lined(relation_acc),
-        lined(edge_src), lined(edge_dst), lined(edge_rel), lined(negatives),
-        lined(ovf_src), lined(ovf_dst), lined(ovf_rel), ovf_count.reshape(1, -1),
-    )
+            collective_id=0, has_side_effects=True, vmem_limit_bytes=60 * 1024 * 1024),
+    )(*args)
+    new_ent, new_ent_acc, new_rel, new_rel_acc = pl.pallas_call(
+        store,
+        out_shape=out_shape,
+        in_specs=[pl.BlockSpec(memory_space=pltpu.HBM)] * 4,
+        out_specs=[pl.BlockSpec(memory_space=pltpu.HBM)] * 4,
+        scratch_shapes=[dma((4,))],
+        compiler_params=pltpu.CompilerParams(vmem_limit_bytes=60 * 1024 * 1024),
+    )(*made)
     return new_ent, new_ent_acc.reshape(-1), new_rel, new_rel_acc.reshape(-1)
 
 

time: 42.9 us -> 61.4 us (1.43)
  Pallas kernels: 33.8 us -> 60.6 us
  local copies, waits for them, and re-layouts: 8.07 us -> 0 us
    pallas_call x1 -> x2, Pallas kernels: 33.8 us -> 60.6 us  [the longest x1 35.5 us: body(): pl.pallas_call(functools.partial(kernel, sizes), out_shape=out_shape, in_...]
    unnamed x28 -> x0, local copies, waits for them, and re-layouts: 8.07 us -> none
where the time goes in v2:
time: 61.4 us; the launch traced here: 61.2 us
  Pallas kernels  60.6 us (99%)
  between operations  0.64 us (1%)
    pallas_call x1, Pallas kernels, body(): pl.pallas_call(functools.partial(kernel, sizes), out_shape=out_shape, in_...  35.5 us
    pallas_call x1, Pallas kernels, body(): pl.pallas_call(store, out_shape=out_shape, in_specs=[pl.BlockSpec(memory_...  25.1 us

profile of v2, /device:TPU:1, one launch (start us, length us, event | category | flops | bytes accessed | tf_op | source)
XLA Modules:
  0.0 61.2 jit_solution(10144824814641050997)
XLA Ops:
  0.6 35.5 %shard_map.147 = (f32[256,256]{1,0:T(8,128)}, f32[2,128]{1,0:T(2,128)}, f32[512,256]{1,0:T(8,128)}, f32[4,128]{1,0:T(4,128)}) custom-call(f32[256,256]{1,0:T(8,128)} %a_ent.1, f32[2,128]{1,0:T(2,128)} %bitcast.20, f32[512,256]{1,0:T(8,128)} %a_rel.1, f32[4,128]{1,0:T(4,128)} %bitcast.18, s32[8,128]{1,0:T(8,128)} %bitcast.12, s32[8,128]{1,0:T(8,128)} %bitcast.13, ...), custom_call_target="tpu_custom_call" | custom-call | tf_op jit(solution)/shard_map/pallas_call | solution.py:465
  36.1 25.1 %shard_map.148 = (f32[256,256]{1,0:T(8,128)}, f32[2,128]{1,0:T(2,128)}, f32[512,256]{1,0:T(8,128)}, f32[4,128]{1,0:T(4,128)}) custom-call(f32[256,256]{1,0:T(8,128)} %get-tuple-element.12.refs_0_, f32[2,128]{1,0:T(2,128)} %get-tuple-element.13.refs_1_, f32[512,256]{1,0:T(8,128)} %get-tuple-element.14.refs_2_, f32[4,128]{1,0:T(4,128)} %get-tuple-element.15.refs_3_), custom_call_target="tpu_custom_call" | custom-call | tf_op jit(solution)/shard_map/pallas_call | solution.py:474

commit v3 on v2

--- a/solution.py
+++ b/solution.py
@@ -180,55 +180,23 @@
     lax.fori_loop(0, edges // CHUNK, score, 0, unroll=True)
 
     mine_r, twin_r = me_s * half_r, other * half_r
-    hop, cut = n_bucket // 2, own_r // 2
-
-    def part(base, k, half=None):
+
+    def part(base, k):
         first = base + around(me_b, k % n_bucket, n_bucket) * own_r
-        if half is None:
-            return pl.ds(pl.multiple_of(first, own_r), own_r)
-        return pl.ds(pl.multiple_of(first + half * cut, cut), cut)
+        return pl.ds(pl.multiple_of(first, own_r), own_r)
 
     def scatter_r(base):
         hot = r_hot[pl.ds(pl.multiple_of(base, half_r), half_r), :]
         return mm(hot, xr_hi[...]) + mm(hot, xr_lo[...])
 
     rel_out[...] = scatter_r(twin_r)
-    order = [hop] + [k * way for k in range(hop - 1, 0, -1) for way in (1, -1)] + [0]
+    order = sorted(range(1, n_bucket), key=lambda k: -min(k, n_bucket - k)) + [0]
     rel_c = {}
     for i, k in enumerate(order):
         copy = remote(rel_out.at[part(0, k)], rel_core.at[part(0, k)], s_rc.at[i], r_rc.at[i],
                       sub=other)
         copy.start()
         rel_c[k] = copy
-    rel_own[...] = scatter_r(mine_r)
-
-    def of_chip(k):
-        rel_c[k].wait_recv()
-        rel_core[part(0, k)] = rel_core[part(0, k)] + rel_own[part(0, k)]
-
-    def toward(way):
-        return around(me_b, 1 if way == 0 else n_bucket - 1, n_bucket)
-
-    rel_z = {}
-
-    def pass_on(way, half, t):
-        k = (hop - t) * (1 if way == 0 else -1)
-        rows = part(0, k, half)
-        if (way, half, t - 1) in rel_z:
-            rel_z[way, half, t - 1].wait_recv()
-            rel_core[rows] = rel_core[rows] + rel_in[way, half, t - 1]
-        copy = remote(rel_core.at[rows], rel_in.at[way, half, t], s_rz.at[way, half, t],
-                      r_rz.at[way, half, t], bucket=toward(way))
-        copy.start()
-        rel_z[way, half, t] = copy
-
-    of_chip(hop)
-    for way in range(2):
-        pass_on(way, way, 0)
-    if hop > 1:
-        for way, k in ((0, hop - 1), (1, 1 - hop)):
-            of_chip(k)
-            pass_on(way, 1 - way, 1)
 
     g_ent[1] = mm(gt_hi[...], q_hi[...]) + mm(gt_hi[...], q_lo[...]) + mm(gt_lo[...], q_hi[...])
     twin_e = pl.ds(pl.multiple_of(other * half_e, half_e), half_e)
@@ -261,39 +229,48 @@
 
     dst_c = to_twin(1)
 
-    if hop > 1:
-        for way in range(2):
-            pass_on(way, way, 1)
-
-    g_ent[0] = mm(s_hot[...], xs_hi[...]) + mm(s_hot[...], xs_lo[...])
-    src_c = to_twin(0)
+    rel_own[...] = scatter_r(mine_r)
+
+    def of_chip(k):
+        rel_c[k].wait_recv()
+        rel_core[part(0, k)] = rel_core[part(0, k)] + rel_own[part(0, k)]
+
+    rel_z = []
+    for k in order[:-1]:
+        of_chip(k)
+        slot = k % n_bucket
+        copy = remote(rel_core.at[part(0, k)], rel_in.at[slot], s_rz.at[slot], r_rz.at[slot],
+                      bucket=around(me_b, slot, n_bucket))
+        copy.start()
+        rel_z.append((slot, copy))
+    of_chip(0)
 
     dst_c.wait_recv()
     ent_core[1] = ent_core[1] + g_ent[1, my_half]
     dst_x = to_rel(1)
-
-    for t in range(2, hop):
-        for way, k in ((0, hop - t), (1, t - hop)):
-            of_chip(k)
-            for half in (way, 1 - way):
-                pass_on(way, half, t)
-    of_chip(0)
-
-    for half in range(2):
-        total = rel_core[part(0, 0, half)]
-        for way in range(2):
-            if (way, half, hop - 1) in rel_z:
-                rel_z[way, half, hop - 1].wait_recv()
-                total = total + rel_in[way, half, hop - 1]
-        rel_all[part(mine_r, 0, half)] = total
-    rel_a, rel_f = {}, []
-
-    def hand_on(way, t):
-        rows = part(mine_r, -t if way == 0 else t, way if t == hop - 1 else None)
-        copy = remote(rel_all.at[rows], rel_all.at[rows], s_ra.at[way, t], r_ra.at[way, t],
-                      bucket=toward(way))
-        copy.start()
-        rel_a[way, t] = copy
+    g_ent[0] = mm(s_hot[...], xs_hi[...]) + mm(s_hot[...], xs_lo[...])
+    src_c = to_twin(0)
+
+    src_c.wait_recv()
+    ent_core[0] = ent_core[0] + g_ent[0, my_half]
+    src_x = to_rel(0)
+
+    share[...] = summed(1, dst_x)
+    moved = remote(share, moved_in, s_mv, r_mv, bucket=around(me_b, 1, n_bucket))
+    moved.start()
+
+    total = rel_core[part(0, 0)]
+    for slot, copy in rel_z:
+        copy.wait_recv()
+        total = total + rel_in[slot]
+    rel_all[part(mine_r, 0)] = total
+    rel_a, rel_f = [], []
+    for k in order[:-1]:
+        slot = k % n_bucket
+        copy = remote(rel_all.at[part(mine_r, 0)], rel_all.at[part(mine_r, 0)], s_ra.at[slot],
+                      r_ra.at[slot], bucket=around(me_b, slot, n_bucket))
+        copy.start()
+        rel_a.append((slot, copy))
 
     def forward_r(rows):
         i = len(rel_f)
@@ -301,23 +278,7 @@
         copy.start()
         rel_f.append(copy)
 
-    for way in range(2):
-        hand_on(way, 0)
     forward_r(part(mine_r, 0))
-
-    src_c.wait_recv()
-    ent_core[0] = ent_core[0] + g_ent[0, my_half]
-    src_x = to_rel(0)
-
-    share[...] = summed(1, dst_x)
-    moved = remote(share, moved_in, s_mv, r_mv, bucket=around(me_b, 1, n_bucket))
-    moved.start()
-
-    for t in range(1, hop):
-        for way in range(2):
-            rel_a[way, t - 1].wait_recv()
-            hand_on(way, t)
-            forward_r(part(mine_r, -t if way == 0 else t))
 
     def rows_e(owner):
         return pl.ds(pl.multiple_of(me_s * half_e + owner * own_e, own_e), own_e)
@@ -341,9 +302,9 @@
 
     forward_e(0)
 
-    for way in range(2):
-        rel_a[way, hop - 1].wait_recv()
-        forward_r(part(mine_r, -hop if way == 0 else hop, way))
+    for slot, copy in reversed(rel_a):
+        copy.wait_recv()
+        forward_r(part(mine_r, -slot))
 
     stores = []
 
@@ -379,7 +340,7 @@
         stores.append(copy)
 
     for copy in [tab, negs, tab_core, dst_c, src_c, moved] + (
-            list(rel_c.values()) + list(rel_z.values()) + list(rel_a.values())
+            list(rel_c.values()) + [copy for _, copy in rel_z + rel_a]
             + dst_x + src_x + rel_f + ent_a + ent_f):
         copy.wait_send()
     for copy in stores:
@@ -387,11 +348,15 @@
 
 
 def store(*refs):
-    sems = refs[-1]
-    copies = [pltpu.make_async_copy(refs[i], refs[4 + i], sems.at[i]) for i in range(4)]
-    for copy in copies:
-        copy.start()
-    for copy in copies:
+    made, out, held, sems = refs[:4], refs[4:8], refs[8:12], refs[12]
+    loads = [pltpu.make_async_copy(made[i], held[i], sems.at[0, i]) for i in range(4)]
+    stores = [pltpu.make_async_copy(held[i], out[i], sems.at[1, i]) for i in range(4)]
+    for load in loads:
+        load.start()
+    for load, copy in zip(loads, stores):
+        load.wait()
+        copy.start()
+    for copy in stores:
         copy.wait()
 
 
@@ -406,7 +371,6 @@
     tiles = edge_src.size // n_sub // LANES + ovf_src.size // LANES
     edges = tiles * LANES
     neg_rows = negatives.size // LANES
-    hop = n_bucket // 2
     vmem = pltpu.VMEM
     dma = pltpu.SemaphoreType.DMA
     args = (
@@ -418,7 +382,7 @@
         vmem((neg_rows, LANES), jnp.int32),
         vmem((ent_rows, width), F32),
         vmem((half_r, width), F32),
-        vmem((2, 2, hop, own_r // 2, width), F32),
+        vmem((n_bucket, own_r, width), F32),
         vmem((rel_rows, width), F32),
         vmem((2, half_e, width), F32),
         vmem((2, n_rel, own_e, width), F32),
@@ -452,9 +416,9 @@
         dma, dma,
         dma((2,)), dma((2,)),
         dma((n_bucket,)), dma((n_bucket,)),
-        dma((2, 2, hop)), dma((2, 2, hop)),
-        dma((2, hop)), dma((2, hop)),
-        dma((n_bucket + 1,)), dma((n_bucket + 1,)),
+        dma((n_bucket,)), dma((n_bucket,)),
+        dma((n_bucket,)), dma((n_bucket,)),
+        dma((n_bucket,)), dma((n_bucket,)),
         dma((2,)), dma((2,)),
         dma((2, n_rel)), dma((2, n_rel)),
         dma, dma,
@@ -476,7 +440,7 @@
         out_shape=out_shape,
         in_specs=[pl.BlockSpec(memory_space=pltpu.HBM)] * 4,
         out_specs=[pl.BlockSpec(memory_space=pltpu.HBM)] * 4,
-        scratch_shapes=[dma((4,))],
+        scratch_shapes=[vmem(arg.shape, F32) for arg in args[:4]] + [dma((2, 4))],
         compiler_params=pltpu.CompilerParams(vmem_limit_bytes=60 * 1024 * 1024),
     )(*made)
     return new_ent, new_ent_acc.reshape(-1), new_rel, new_rel_acc.reshape(-1)

time: 61.4 us -> 35.6 us (0.58)
  Pallas kernels: 60.6 us -> 34.8 us
    pallas_call x1, Pallas kernels: 25.1 us -> 1.99 us  [body(): pl.pallas_call(store, out_shape=out_shape, in_specs=[pl.BlockSpec(memory_...]
    pallas_call x1, Pallas kernels: 35.5 us -> 32.8 us  [body(): pl.pallas_call(functools.partial(kernel, sizes), out_shape=out_shape, in_...]
where the time goes in v3:
time: 35.6 us; the launch traced here: 35.5 us
  Pallas kernels  34.8 us (98%)
  between operations  0.64 us (2%)
    pallas_call x1, Pallas kernels, body(): pl.pallas_call(functools.partial(kernel, sizes), out_shape=out_shape, in_...  32.8 us
    pallas_call x1, Pallas kernels, body(): pl.pallas_call(store, out_shape=out_shape, in_specs=[pl.BlockSpec(memory_...  1.99 us

profile of v3, /device:TPU:1, one launch (start us, length us, event | category | flops | bytes accessed | tf_op | source)
XLA Modules:
  0.0 35.5 jit_solution(6266564670162228896)
XLA Ops:
  0.6 32.8 %shard_map.147 = (f32[256,256]{1,0:T(8,128)}, f32[2,128]{1,0:T(2,128)}, f32[512,256]{1,0:T(8,128)}, f32[4,128]{1,0:T(4,128)}) custom-call(f32[256,256]{1,0:T(8,128)} %a_ent.1, f32[2,128]{1,0:T(2,128)} %bitcast.20, f32[512,256]{1,0:T(8,128)} %a_rel.1, f32[4,128]{1,0:T(4,128)} %bitcast.18, s32[8,128]{1,0:T(8,128)} %bitcast.12, s32[8,128]{1,0:T(8,128)} %bitcast.13, ...), custom_call_target="tpu_custom_call" | custom-call | tf_op jit(solution)/shard_map/pallas_call | solution.py:429
  33.5 2.0 %shard_map.148 = (f32[256,256]{1,0:T(8,128)}, f32[2,128]{1,0:T(2,128)}, f32[512,256]{1,0:T(8,128)}, f32[4,128]{1,0:T(4,128)}) custom-call(f32[256,256]{1,0:T(8,128)} %get-tuple-element.12.refs_0_, f32[2,128]{1,0:T(2,128)} %get-tuple-element.13.refs_1_, f32[512,256]{1,0:T(8,128)} %get-tuple-element.14.refs_2_, f32[4,128]{1,0:T(4,128)} %get-tuple-element.15.refs_3_), custom_call_target="tpu_custom_call" | custom-call | tf_op jit(solution)/shard_map/pallas_call | solution.py:438

commit v4 on v3

--- a/solution.py
+++ b/solution.py
@@ -140,7 +140,7 @@
         r_hot[:, rows] = (sub_r == r_id).astype(F32).astype(BF16)
         return carry
 
-    lax.fori_loop(0, tiles, gather, 0)
+    lax.fori_loop(0, tiles, gather, 0, unroll=True)
 
     negs.wait_recv()
     times = jnp.zeros((1, ent_rows), F32)

time: 35.6 us -> 33.9 us (0.952)
  Pallas kernels: 34.8 us -> 33.1 us
    pallas_call x1, Pallas kernels: 32.8 us -> 31.1 us  [body(): pl.pallas_call(functools.partial(kernel, sizes), out_shape=out_shape, in_...]
where the time goes in v4:
time: 33.9 us; the launch traced here: 33.8 us
  Pallas kernels  33.1 us (98%)
  between operations  0.64 us (2%)
    pallas_call x1, Pallas kernels, body(): pl.pallas_call(functools.partial(kernel, sizes), out_shape=out_shape, in_...  31.1 us
    pallas_call x1, Pallas kernels, body(): pl.pallas_call(store, out_shape=out_shape, in_specs=[pl.BlockSpec(memory_...  1.99 us

profile of v4, /device:TPU:1, one launch (start us, length us, event | category | flops | bytes accessed | tf_op | source)
XLA Modules:
  0.0 33.8 jit_solution(14185090005620883577)
XLA Ops:
  0.6 31.1 %shard_map.147 = (f32[256,256]{1,0:T(8,128)}, f32[2,128]{1,0:T(2,128)}, f32[512,256]{1,0:T(8,128)}, f32[4,128]{1,0:T(4,128)}) custom-call(f32[256,256]{1,0:T(8,128)} %a_ent.1, f32[2,128]{1,0:T(2,128)} %bitcast.20, f32[512,256]{1,0:T(8,128)} %a_rel.1, f32[4,128]{1,0:T(4,128)} %bitcast.18, s32[8,128]{1,0:T(8,128)} %bitcast.12, s32[8,128]{1,0:T(8,128)} %bitcast.13, ...), custom_call_target="tpu_custom_call" | custom-call | tf_op jit(solution)/shard_map/pallas_call | solution.py:429
  31.8 2.0 %shard_map.148 = (f32[256,256]{1,0:T(8,128)}, f32[2,128]{1,0:T(2,128)}, f32[512,256]{1,0:T(8,128)}, f32[4,128]{1,0:T(4,128)}) custom-call(f32[256,256]{1,0:T(8,128)} %get-tuple-element.12.refs_0_, f32[2,128]{1,0:T(2,128)} %get-tuple-element.13.refs_1_, f32[512,256]{1,0:T(8,128)} %get-tuple-element.14.refs_2_, f32[4,128]{1,0:T(4,128)} %get-tuple-element.15.refs_3_), custom_call_target="tpu_custom_call" | custom-call | tf_op jit(solution)/shard_map/pallas_call | solution.py:438
